TPU v7x, 32 devices: a whole 2x2x4 slice. The times are simulated.
32 devices in a mesh: dp: 8 (over y, x, core), tensor: 4 (over z).
Axes of the slice: x: 2, y: 2, z: 4, core: 2. Of those that a mesh axis runs over, the one named last changes fastest.
Arguments:
- tokens: bfloat16 [16384, 1024], P(('dp', 'tensor')), may hold values from -6 to 6
- w_qkv: bfloat16 [1024, 3, 1024], P('dp', None, 'tensor'), may hold values from -0.25 to 0.25
- w_out: bfloat16 [1024, 1024], P('tensor', 'dp'), may hold values from -0.5 to 0.5
- w_in: bfloat16 [1024, 2, 2624], P('dp', None, 'tensor'), may hold values from -0.1875 to 0.1875
- w_down: bfloat16 [2624, 1024], P('tensor', 'dp'), may hold values from -0.125 to 0.125
- gain_attn: bfloat16 [1024], P('dp'), may hold values from 0.5 to 1.5
- gain_mlp: bfloat16 [1024], P('dp'), may hold values from 0.5 to 1.5
- grad_output: bfloat16 [16384, 1024], P(('dp', 'tensor')), may hold values from -6 to 6
Outputs:
- output: bfloat16 [16384, 1024], P(('dp', 'tensor'))
- grad_tokens: bfloat16 [16384, 1024], P(('dp', 'tensor'))
- grad_qkv: float32 [1024, 3, 1024], P('dp', None, 'tensor')
- grad_out: float32 [1024, 1024], P('tensor', 'dp')
- grad_in: float32 [1024, 2, 2624], P('dp', None, 'tensor')
- grad_down: float32 [2624, 1024], P('tensor', 'dp')
- grad_gain_attn: float32 [1024], P('dp')
- grad_gain_mlp: float32 [1024], P('dp')
All inputs are finite; a program needn't handle non-finite values.
Results may differ from a plain program's by a relative error of at most 0.017.
The roundings to bfloat16 on the way count: a program that leaves them out, or rounds other values in their place, can miss the bound.
Values may be sent and summed in bfloat16 or wider, within the bound.
A program may use at most 192 MiB of HBM per device.

v0:
```python
import jax
import jax.numpy as jnp
from jax import lax
from jax.sharding import PartitionSpec as P

HD = 64
LEN = 1024
EPS = 1e-05
THETA = 160000.0


def layer_norm(values, gain):
    centred = values - jnp.mean(values, axis=-1, keepdims=True)
    spread = jnp.mean(centred * centred, axis=-1, keepdims=True)
    return centred * lax.rsqrt(spread + EPS) * gain


def rotary(values, length):
    rows = values.shape[0]
    half = values.shape[-1] // 2
    freq = THETA ** (-(jnp.arange(half).astype(jnp.float32) * 2.0 / values.shape[-1]))
    place = (jnp.arange(rows) % length).astype(jnp.float32)
    angle = place[:, None] * freq[None, :]
    cosine = jnp.cos(angle)[:, None, :]
    sine = jnp.sin(angle)[:, None, :]
    first = values[..., :half]
    second = values[..., half:]
    return jnp.concatenate(
        [first * cosine - second * sine, second * cosine + first * sine], axis=-1
    )


def geglu(pair):
    return jax.nn.gelu(pair[:, 0], approximate=False) * pair[:, 1]


def rotate_seq(values):
    return rotary(values, LEN)


def attend(query, key, value, length):
    rows, heads, size = query.shape
    block = min(512, length)
    scale = size ** (-0.5)

    def single(index):
        start = index * block
        first = start // length * length
        query_block = lax.dynamic_slice_in_dim(query, start, block, 0)
        key_seq = lax.dynamic_slice_in_dim(key, first, length, 0)
        value_seq = lax.dynamic_slice_in_dim(value, first, length, 0)
        scores = (
            jnp.einsum("qhe,khe->hqk", query_block, key_seq, preferred_element_type=jnp.float32)
            * scale
        )
        highest = jnp.max(scores, axis=-1, keepdims=True)
        total = jnp.sum(jnp.exp(scores - highest), axis=-1, keepdims=True)
        lse = highest + jnp.log(total)
        probs = jnp.exp(scores - lse).astype(jnp.bfloat16)
        result = jnp.einsum("hqk,khe->qhe", probs, value_seq, preferred_element_type=jnp.float32)
        return (result, lse[..., 0])

    results, lses = lax.map(single, jnp.arange(rows // block))
    return (results.reshape(rows, heads, size), lses)


def attend_back(query, key, value, lses, grad_att, length):
    rows, heads, size = query.shape
    block = min(512, length)
    scale = size ** (-0.5)
    zeros = jnp.zeros((rows, heads, size), jnp.float32)

    def step(index, carry):
        grad_query, grad_key, grad_value = carry
        start = index * block
        first = start // length * length
        query_block = lax.dynamic_slice_in_dim(query, start, block, 0)
        grad_block = lax.dynamic_slice_in_dim(grad_att, start, block, 0)
        key_seq = lax.dynamic_slice_in_dim(key, first, length, 0)
        value_seq = lax.dynamic_slice_in_dim(value, first, length, 0)
        lse = lax.dynamic_index_in_dim(lses, index, 0, keepdims=False)
        scores = (
            jnp.einsum("qhe,khe->hqk", query_block, key_seq, preferred_element_type=jnp.float32)
            * scale
        )
        probs = jnp.exp(scores - lse[..., None])
        dprob = jnp.einsum(
            "qhe,khe->hqk", grad_block, value_seq, preferred_element_type=jnp.float32
        )
        inner = jnp.sum(dprob * probs, axis=-1, keepdims=True)
        grad_scores = (probs * (dprob - inner)).astype(jnp.bfloat16)
        part_query = (
            jnp.einsum("hqk,khe->qhe", grad_scores, key_seq, preferred_element_type=jnp.float32)
            * scale
        )
        part_key = (
            jnp.einsum("hqk,qhe->khe", grad_scores, query_block, preferred_element_type=jnp.float32)
            * scale
        )
        part_value = jnp.einsum(
            "hqk,qhe->khe",
            probs.astype(jnp.bfloat16),
            grad_block,
            preferred_element_type=jnp.float32,
        )
        grad_query = lax.dynamic_update_slice_in_dim(grad_query, part_query, start, 0)
        grad_key = lax.dynamic_update_slice_in_dim(
            grad_key, lax.dynamic_slice_in_dim(grad_key, first, length, 0) + part_key, first, 0
        )
        grad_value = lax.dynamic_update_slice_in_dim(
            grad_value,
            lax.dynamic_slice_in_dim(grad_value, first, length, 0) + part_value,
            first,
            0,
        )
        return (grad_query, grad_key, grad_value)

    return lax.fori_loop(0, rows // block, step, (zeros, zeros, zeros))


def local(tokens, w_qkv, w_out, w_in, w_down, gain_attn, gain_mlp, grad_output):
    gathered_w = (
        lax.all_gather(w_qkv, "dp", axis=0, tiled=True),
        lax.all_gather(w_out, "dp", axis=1, tiled=True),
        lax.all_gather(w_in, "dp", axis=0, tiled=True),
        lax.all_gather(w_down, "dp", axis=1, tiled=True),
        lax.all_gather(gain_attn, "dp", axis=0, tiled=True),
        lax.all_gather(gain_mlp, "dp", axis=0, tiled=True),
    )
    qkv_w, out_w, in_w, down_w, gain_first, gain_second = gathered_w
    gain_one = gain_first.astype(jnp.float32)
    gain_two = gain_second.astype(jnp.float32)
    inputs = tokens.astype(jnp.float32)
    normed_one = layer_norm(inputs, gain_one).astype(jnp.bfloat16)
    gathered_one = lax.all_gather(normed_one, "tensor", axis=0, tiled=True)
    rows = gathered_one.shape[0]
    heads = qkv_w.shape[2] // HD
    projected = jnp.einsum("td,dcf->tcf", gathered_one, qkv_w, preferred_element_type=jnp.float32)
    split = projected.reshape(rows, 3, heads, HD)
    query_f = split[:, 0]
    query_b = rotary(query_f, LEN).astype(jnp.bfloat16)
    key_b = rotary(split[:, 1], LEN).astype(jnp.bfloat16)
    value_b = split[:, 2].astype(jnp.bfloat16)
    attended, lses = attend(query_b, key_b, value_b, LEN)
    attended_b = attended.reshape(rows, heads * HD).astype(jnp.bfloat16)
    branch_one = lax.psum_scatter(
        jnp.dot(attended_b, out_w, preferred_element_type=jnp.float32),
        "tensor",
        scatter_dimension=0,
        tiled=True,
    )
    residual = inputs + branch_one
    normed_two = layer_norm(residual, gain_two).astype(jnp.bfloat16)
    gathered_two = lax.all_gather(normed_two, "tensor", axis=0, tiled=True)
    pair = jnp.einsum("td,dcf->tcf", gathered_two, in_w, preferred_element_type=jnp.float32)
    hidden = geglu(pair).astype(jnp.bfloat16)
    branch_two = lax.psum_scatter(
        jnp.dot(hidden, down_w, preferred_element_type=jnp.float32).astype(jnp.bfloat16),
        "tensor",
        scatter_dimension=0,
        tiled=True,
    ).astype(jnp.float32)
    output = (residual + branch_two).astype(jnp.bfloat16)
    regathered = (
        lax.all_gather(w_qkv, "dp", axis=0, tiled=True),
        lax.all_gather(w_out, "dp", axis=1, tiled=True),
        lax.all_gather(w_in, "dp", axis=0, tiled=True),
        lax.all_gather(w_down, "dp", axis=1, tiled=True),
        lax.all_gather(gain_attn, "dp", axis=0, tiled=True),
        lax.all_gather(gain_mlp, "dp", axis=0, tiled=True),
    )
    qkv_w, out_w, in_w, down_w, gain_first, gain_second = regathered
    gain_one = gain_first.astype(jnp.float32)
    gain_two = gain_second.astype(jnp.float32)
    grad_top = grad_output.astype(jnp.float32)
    grad_all = lax.all_gather(grad_output, "tensor", axis=0, tiled=True)
    grad_down = jnp.einsum("tf,td->fd", hidden, grad_all, preferred_element_type=jnp.float32)
    grad_hidden = jnp.einsum("td,fd->tf", grad_all, down_w, preferred_element_type=jnp.float32)
    geglu_pull = jax.vjp(geglu, pair)[1]
    grad_pair = geglu_pull(grad_hidden)[0].astype(jnp.bfloat16)
    grad_in = jnp.einsum("td,tcf->dcf", gathered_two, grad_pair, preferred_element_type=jnp.float32)
    grad_normed_two = lax.psum_scatter(
        jnp.einsum("tcf,dcf->td", grad_pair, in_w, preferred_element_type=jnp.float32),
        "tensor",
        scatter_dimension=0,
        tiled=True,
    )
    norm_pull_two = jax.vjp(layer_norm, residual, gain_two)[1]
    grad_res_part, grad_gain_two = norm_pull_two(grad_normed_two)
    grad_residual = grad_top + grad_res_part
    grad_res_b = grad_residual.astype(jnp.bfloat16)
    grad_res_all = lax.all_gather(grad_res_b, "tensor", axis=0, tiled=True)
    grad_out_w = jnp.einsum(
        "tf,td->fd", attended_b, grad_res_all, preferred_element_type=jnp.float32
    )
    grad_att = jnp.einsum("td,fd->tf", grad_res_all, out_w, preferred_element_type=jnp.float32)
    grad_att = grad_att.astype(jnp.bfloat16).reshape(rows, heads, HD)
    grad_query, grad_key, grad_value = attend_back(query_b, key_b, value_b, lses, grad_att, LEN)
    rotary_pull = jax.vjp(rotate_seq, query_f)[1]
    back_query = rotary_pull(grad_query)[0]
    back_key = rotary_pull(grad_key)[0]
    grad_proj = (
        jnp.stack([back_query, back_key, grad_value], axis=1)
        .reshape(rows, 3, heads * HD)
        .astype(jnp.bfloat16)
    )
    grad_qkv_w = jnp.einsum(
        "td,tcf->dcf", gathered_one, grad_proj, preferred_element_type=jnp.float32
    )
    grad_normed_one = lax.psum_scatter(
        jnp.einsum("tcf,dcf->td", grad_proj, qkv_w, preferred_element_type=jnp.float32),
        "tensor",
        scatter_dimension=0,
        tiled=True,
    )
    norm_pull_one = jax.vjp(layer_norm, inputs, gain_one)[1]
    grad_in_part, grad_gain_one = norm_pull_one(grad_normed_one)
    grad_tokens = (grad_residual + grad_in_part).astype(jnp.bfloat16)
    summed = (
        lax.psum_scatter(grad_qkv_w, "dp", scatter_dimension=0, tiled=True),
        lax.psum_scatter(grad_out_w, "dp", scatter_dimension=1, tiled=True),
        lax.psum_scatter(grad_in, "dp", scatter_dimension=0, tiled=True),
        lax.psum_scatter(grad_down, "dp", scatter_dimension=1, tiled=True),
        lax.psum_scatter(grad_gain_one, "dp", scatter_dimension=0, tiled=True),
        lax.psum_scatter(grad_gain_two, "dp", scatter_dimension=0, tiled=True),
    )
    gain_first_grad, gain_second_grad = lax.psum((summed[4], summed[5]), "tensor")
    return (
        output,
        grad_tokens,
        summed[0],
        summed[1],
        summed[2],
        summed[3],
        gain_first_grad,
        gain_second_grad,
    )


def solution(mesh):
    placed = (
        P(("dp", "tensor"), None),
        P("dp", None, "tensor"),
        P("tensor", "dp"),
        P("dp", None, "tensor"),
        P("tensor", "dp"),
        P("dp"),
        P("dp"),
        P(("dp", "tensor"), None),
    )
    return jax.shard_map(
        local,
        mesh=mesh,
        in_specs=placed,
        out_specs=(
            P(("dp", "tensor"), None),
            P(("dp", "tensor"), None),
            P("dp", None, "tensor"),
            P("tensor", "dp"),
            P("dp", None, "tensor"),
            P("tensor", "dp"),
            P("dp"),
            P("dp"),
        ),
        check_vma=False,
    )
```

profile of v0, /device:TPU:0, one launch (start us, length us, event | category | flops | bytes accessed | tf_op | source)
XLA Modules:
  0.0 1317.4 jit_solution(13067545842820573546)
XLA Ops:
  9.0 10.3 all-gather
  26.4 12.3 all_gather.39
  40.5 82.9 %all-gather.10.cloned.1.call-done = bf16[2048,1024]{1,0:T(8,128)(2,1)} async-done(((bf16[512,1024]{1,0:T(8,128)(2,1)}), bf16[2048,1024]{1,0:T(8,128)(2,1)}) %all-gather.10.cloned.1.call-update) | async-done | bytes 4194320 | tf_op jit(solution)/shard_map/all_gather | solution.py:135
  130.6 29.7 %while.33 = (s32[]{:T(128)}, bf16[4,512,4,64]{1,3,2,0:T(8,128)(2,1)}, f32[4,4,512]{2,1,0:T(4,128)S(1)}, s32[4]{0:T(128)S(1)}, bf16[2048,4,64]{0,2,1:T(8,128)(2,1...) while((s32[]{:T(128)}, ...), condition=%wide.region_5.6_spmd, body=%wide.region_2.5_spmd.sunk | while | flops 553646080 | bytes 35455444 | solution.py:63
  179.8 132.3 %reduce-scatter.9.cloned.1.call-done = f32[512,1024]{1,0:T(8,128)} async-done(((f32[2048,1024]{1,0:T(8,128)}), f32[512,1024]{1,0:T(8,128)}) %reduce-scatter.9.cloned.1.call-update) | async-done | bytes 2097168 | tf_op jit(solution)/shard_map/reduce_scatter | solution.py:146
  316.0 23.5 %all-gather.18.cloned.1.call-done = bf16[656,1024]{1,0:T(8,128)(2,1)} async-done(((bf16[656,128]{1,0:T(8,128)(2,1)}), bf16[656,1024]{1,0:T(8,128)(2,1)}) %all-gather.18.cloned.1.call-update) | async-done | bytes 1343504 | tf_op jit(solution)/shard_map/all_gather | solution.py:126
  339.5 82.2 %all-gather.20.cloned.1.call-done = bf16[2048,1024]{1,0:T(8,128)(2,1)} async-done(((bf16[512,1024]{1,0:T(8,128)(2,1)}), bf16[2048,1024]{1,0:T(8,128)(2,1)}) %all-gather.20.cloned.1.call-update) | async-done | bytes 4194320 | tf_op jit(solution)/shard_map/all_gather | solution.py:176
  429.7 23.2 %all-gather.16.cloned.1.call-done = bf16[1024,2,656]{0,2,1:T(8,128)(2,1)} async-done(((bf16[128,2,656]{0,2,1:T(8,128)(2,1)}), bf16[1024,2,656]{0,2,1:T(8,128)(2,1)}) %all-gather.16.cloned.1.call-update) | async-done | bytes 2686992 | tf_op jit(solution)/shard_map/all_gather | solution.py:125
  452.8 82.9 %all-gather.14.cloned.1.call-done = bf16[2048,1024]{1,0:T(8,128)(2,1)} async-done(((bf16[512,1024]{1,0:T(8,128)(2,1)}), bf16[2048,1024]{1,0:T(8,128)(2,1)}) %all-gather.14.cloned.1.call-update) | async-done | bytes 4194320 | tf_op jit(solution)/shard_map/all_gather | solution.py:154
  544.3 12.5 multiply_bitcast_fusion
  562.0 13.5 %convolution_bitcast_fusion.1 = f32[2048,1024]{1,0:T(8,128)} fusion(bf16[1024,2,656]{0,2,1:T(8,128)(2,1)} %all-gather.16.cloned.1.call-done, f32[2048,1,656]{0,2,1:T(8,128)} %get-tuple-element.379, f32[2048,1,656]{0,2,1:T(8,128)} %get-tuple-element.371), kind=kOutput, calls=%fused_computation.82 | convolution fusion | flops 5508300800 | bytes 21823488 | tf_op jit(solution)/shard_map/tcf,dcf->td/dot_general | solution.py:183
  575.6 11.9 reduce-scatter.11.cloned.1.call-start
  595.2 123.5 %reduce-scatter.13.cloned.1.call-done = f32[512,1024]{1,0:T(8,128)} async-done(((f32[2048,1024]{1,0:T(8,128)}), f32[512,1024]{1,0:T(8,128)}) %reduce-scatter.13.cloned.1.call-update) | async-done | bytes 2097168 | tf_op jit(solution)/shard_map/reduce_scatter | solution.py:182
  721.6 77.0 %reduce-scatter.11.cloned.1.call-done = bf16[512,1024]{1,0:T(8,128)(2,1)} async-done(((bf16[2048,1024]{1,0:T(8,128)(2,1)}), bf16[512,1024]{1,0:T(8,128)(2,1)}) %reduce-scatter.11.cloned.1.call-update) | async-done | bytes 1048592 | tf_op jit(solution)/shard_map/reduce_scatter | solution.py:157
  805.0 81.4 %all-gather.22.cloned.1.call-done = bf16[2048,1024]{1,0:T(8,128)(2,1)} async-done(((bf16[512,1024]{1,0:T(8,128)(2,1)}), bf16[2048,1024]{1,0:T(8,128)(2,1)}) %all-gather.22.cloned.1.call-update) | async-done | bytes 4194320 | tf_op jit(solution)/shard_map/all_gather | solution.py:192
  894.2 53.7 %while.34 = (s32[]{:T(128)}, f32[2048,4,64]{0,2,1:T(8,128)}, f32[2048,4,64]{0,2,1:T(8,128)S(1)}, f32[2048,4,64]{0,2,1:T(8,128)}, bf16[2048,4,64]{0,2,1:T(8,128)(...) while((s32[]{:T(128)}, f32[2048,4,64]{0,2,1:T(8,128)}, ...), condition=%wide.region_15.16_spmd, body=%wide.region_13.15_spmd.sunk | while | flops 1368258560 | bytes 95478312 | solution.py:118
  974.0 11.2 fusion.64
  1000.1 108.7 %reduce-scatter.15.cloned.1.call-done = f32[512,1024]{1,0:T(8,128)} async-done(((f32[2048,1024]{1,0:T(8,128)}), f32[512,1024]{1,0:T(8,128)}) %reduce-scatter.15.cloned.1.call-update) | async-done | bytes 2097168 | tf_op jit(solution)/shard_map/reduce_scatter | solution.py:210
  1112.1 13.7 %all-reduce.8 = (f32[1024]{0:T(1024)S(1)}, f32[1024]{0:T(1024)S(1)}) all-reduce(f32[1024]{0:T(1024)S(1)} %get-tuple-element.329, f32[1024]{0:T(1024)S(1)} %copy-done.37), channel_id=10, replica_groups=mesh['dp'=8,'tensor'=4] {'dp'}, use_global_device_ids=true, to_apply=%region_24.25.clone | all-reduce | flops 2048 | bytes 16384
  1125.9 12.1 all-reduce.9
  1141.3 17.2 %reduce-scatter.23.cloned.1.call-done = f32[656,128]{1,0:T(8,128)} async-done(((f32[656,1024]{1,0:T(8,128)}), f32[656,128]{1,0:T(8,128)}) %reduce-scatter.23.cloned.1.call-update) | async-done | bytes 335888 | tf_op jit(solution)/shard_map/reduce_scatter | solution.py:223
  1158.5 61.6 %reduce-scatter.21.cloned.1.call-done = f32[128,2,656]{0,2,1:T(8,128)} async-done(((f32[1024,2,656]{0,2,1:T(8,128)}), f32[128,2,656]{0,2,1:T(8,128)}) %reduce-scatter.21.cloned.1.call-update) | async-done | bytes 671760 | tf_op jit(solution)/shard_map/reduce_scatter | solution.py:222
  1220.1 40.0 %reduce-scatter.19.cloned.1.call-done = f32[256,128]{1,0:T(8,128)} async-done(((f32[256,1024]{1,0:T(8,128)}), f32[256,128]{1,0:T(8,128)}) %reduce-scatter.19.cloned.1.call-update) | async-done | bytes 131088 | tf_op jit(solution)/shard_map/reduce_scatter | solution.py:221
  1260.1 50.5 %reduce-scatter.17.cloned.1.call-done = f32[128,3,256]{2,0,1:T(8,128)} async-done(((f32[1024,3,256]{2,0,1:T(8,128)}), f32[128,3,256]{2,0,1:T(8,128)}) %reduce-scatter.17.cloned.1.call-update) | async-done | bytes 393232 | tf_op jit(solution)/shard_map/reduce_scatter | solution.py:220
  (254 shorter events, 214.4 us)
Async XLA Ops:
  7.2 33.4 %all-gather.12.cloned.1.call-start = ((), (), s32[]{:S(2)}) async-start(), calls=%async_computation.9 | async-start | bytes 1769472 | tf_op jit(solution)/shard_map/all_gather | solution.py:123
  9.0 114.4 %all-gather.10.cloned.1.call-start = ((), (), s32[]{:S(2)}) async-start(), calls=%async_computation.8 | async-start | bytes 5242880 | tf_op jit(solution)/shard_map/all_gather | solution.py:135
  26.3 285.9 %reduce-scatter.9.cloned.1.call-start = ((), (), s32[]{:S(2)}) async-start(), calls=%async_computation.10 | async-start | bytes 10485760 | tf_op jit(solution)/shard_map/reduce_scatter | solution.py:146
  39.7 90.1 %copy-start.16 = (f32[2048,32]{0,1:T(8,128)}, f32[2048,32]{0,1:T(8,128)S(1)}, u32[]{:S(2)}) copy-start(f32[2048,32]{0,1:T(8,128)S(1)} %get-tuple-element.396) | copy-start | bytes 786436
  169.0 170.5 %all-gather.18.cloned.1.call-start = ((), (), s32[]{:S(2)}) async-start(), calls=%async_computation.13 | async-start | bytes 1511424 | tf_op jit(solution)/shard_map/all_gather | solution.py:126
  169.6 252.1 %all-gather.20.cloned.1.call-start = ((), (), s32[]{:S(2)}) async-start(), calls=%async_computation.15 | async-start | bytes 5242880 | tf_op jit(solution)/shard_map/all_gather | solution.py:176
  170.2 282.6 %all-gather.16.cloned.1.call-start = ((), (), s32[]{:S(2)}) async-start(), calls=%async_computation.12 | async-start | bytes 3022848 | tf_op jit(solution)/shard_map/all_gather | solution.py:125
  170.8 365.0 %all-gather.14.cloned.1.call-start = ((), (), s32[]{:S(2)}) async-start(), calls=%async_computation.11 | async-start | bytes 5242880 | tf_op jit(solution)/shard_map/all_gather | solution.py:154
  316.0 402.7 %reduce-scatter.13.cloned.1.call-start = ((), (), s32[]{:S(2)}) async-start(), calls=%async_computation.16 | async-start | bytes 10485760 | tf_op jit(solution)/shard_map/reduce_scatter | solution.py:182
  575.6 223.0 %reduce-scatter.11.cloned.1.call-start = ((), (), s32[]{:S(2)}) async-start(), calls=%async_computation.14 | async-start | bytes 5242880 | tf_op jit(solution)/shard_map/reduce_scatter | solution.py:157
  595.2 291.2 %all-gather.22.cloned.1.call-start = ((), (), s32[]{:S(2)}) async-start(), calls=%async_computation.17 | async-start | bytes 5242880 | tf_op jit(solution)/shard_map/all_gather | solution.py:192
  804.9 303.9 %reduce-scatter.15.cloned.1.call-start = ((), (), s32[]{:S(2)}) async-start(), calls=%async_computation.18 | async-start | bytes 10485760 | tf_op jit(solution)/shard_map/reduce_scatter | solution.py:210
  965.6 192.8 %reduce-scatter.23.cloned.1.call-start = ((), (), s32[]{:S(2)}) async-start(), calls=%async_computation.22 | async-start | bytes 3022848 | tf_op jit(solution)/shard_map/reduce_scatter | solution.py:223
  974.0 246.1 %reduce-scatter.21.cloned.1.call-start = ((), (), s32[]{:S(2)}) async-start(), calls=%async_computation.21 | async-start | bytes 6045696 | tf_op jit(solution)/shard_map/reduce_scatter | solution.py:222
  985.3 274.8 %reduce-scatter.19.cloned.1.call-start = ((), (), s32[]{:S(2)}) async-start(), calls=%async_computation.20 | async-start | bytes 1179648 | tf_op jit(solution)/shard_map/reduce_scatter | solution.py:221
  990.9 117.9 %copy-start = (bf16[512,1024]{1,0:T(8,128)(2,1)S(1)}, bf16[512,1024]{1,0:T(8,128)(2,1)}, u32[]{:S(2)}) copy-start(bf16[512,1024]{1,0:T(8,128)(2,1)} %param.12) | copy-start | bytes 3145732
  990.9 117.9 %copy-start.27 = (f32[8,1,128]{2,1,0:T(1,128)S(1)}, f32[8,1,128]{2,1,0:T(1,128)}, u32[]{:S(2)}) copy-start(f32[8,1,128]{2,1,0:T(1,128)} %copy-done.26) | copy-start | bytes 12292
  990.9 117.9 %copy-start.29 = (f32[512]{0:T(512)S(1)}, f32[512]{0:T(512)}, u32[]{:S(2)}) copy-start(f32[512]{0:T(512)} %copy-done.28) | copy-start | bytes 6148
  990.9 319.6 %reduce-scatter.17.cloned.1.call-start = ((), (), s32[]{:S(2)}) async-start(), calls=%async_computation.19 | async-start | bytes 3538944 | tf_op jit(solution)/shard_map/reduce_scatter | solution.py:220
  998.7 112.3 %copy-start.36 = (f32[512]{0:T(512)S(1)}, f32[512]{0:T(512)}, u32[]{:S(2)}) copy-start(f32[512]{0:T(512)} %copy-done.35) | copy-start | bytes 6148
  998.7 112.3 %copy-start.32 = (f32[512]{0:T(512)S(1)}, f32[512]{0:T(512)}, u32[]{:S(2)}) copy-start(f32[512]{0:T(512)} %copy-done.31) | copy-start | bytes 6148
  998.7 113.4 %copy-start.37 = (f32[1024]{0:T(1024)S(1)}, f32[1024]{0:T(1024)}, u32[]{:S(2)}) copy-start(f32[1024]{0:T(1024)} %get-tuple-element.327) | copy-start | bytes 12292
  998.7 139.3 %copy-start.8 = (f32[512,1024]{1,0:T(8,128)S(1)}, f32[512,1024]{1,0:T(8,128)}, u32[]{:S(2)}) copy-start(f32[512,1024]{1,0:T(8,128)} %copy-done.7) | copy-start | bytes 6291460
  998.7 139.3 %copy-start.34 = (f32[512]{0:T(512)S(1)}, f32[512]{0:T(512)}, u32[]{:S(2)}) copy-start(f32[512]{0:T(512)} %copy-done.33) | copy-start | bytes 6148
  (49 other events, 416.2 us)
Sparse Core Ops, SparseCore 0:
  10.5 30.0 all-gather.11
  42.7 80.7 all-gather.9
  169.1 142.9 reduce-scatter.8
  313.9 25.5 all-gather.17
  340.9 80.7 all-gather.19
  423.5 29.3 all-gather.15
  455.0 80.7 all-gather.13
  575.7 142.9 reduce-scatter.12
  721.0 77.4 reduce-scatter.10
  805.0 81.2 all-gather.21
  965.7 142.9 reduce-scatter.14
  1113.0 45.3 reduce-scatter.22
  1162.8 57.1 reduce-scatter.20
  1224.0 36.0 reduce-scatter.18
  1264.3 46.2 reduce-scatter.16
where the time goes:
time: 1330 us; the launch traced here: 1320 us
  waiting for transfers between devices  989 us (74%)
  matrix products  150 us (11%)
  other arithmetic  64.2 us (5%)
  blocking collectives  57.4 us (4%)
  local copies, waits for them, and re-layouts  25.2 us (2%)
  between operations  15.4 us (1%)
    reduce_scatter x1, waiting for transfers between devices, local(): lax.psum_scatter(jnp.dot(attended_b, out_w, preferred_element_type=jnp.fl...  132 us
    reduce_scatter x1, waiting for transfers between devices, local(): lax.psum_scatter(jnp.einsum('tcf,dcf->td', grad_pair, in_w, preferred_ele...  124 us
    reduce_scatter x1, waiting for transfers between devices, local(): lax.psum_scatter(jnp.einsum('tcf,dcf->td', grad_proj, qkv_w, preferred_el...  109 us
    all_gather x1, waiting for transfers between devices, local(): gathered_two = lax.all_gather(normed_two, 'tensor', axis=0, tiled=True)  82.9 us
    all_gather x1, waiting for transfers between devices, local(): gathered_one = lax.all_gather(normed_one, 'tensor', axis=0, tiled=True)  82.9 us
    all_gather x1, waiting for transfers between devices, local(): grad_all = lax.all_gather(grad_output, 'tensor', axis=0, tiled=True)  82.2 us
    all_gather x1, waiting for transfers between devices, local(): grad_res_all = lax.all_gather(grad_res_b, 'tensor', axis=0, tiled=True)  81.4 us
    reduce_scatter x1, waiting for transfers between devices, local(): lax.psum_scatter(jnp.dot(hidden, down_w, preferred_element_type=jnp.float...  77 us
  transfers between devices with their start and end apart: 15, of which 15 were waited for; matrix products, arithmetic and copies ran while one was open for 5% of the time, Pallas kernels for 0%

commit v1 on v0

--- a/solution.py
+++ b/solution.py
@@ -7,6 +7,22 @@
 LEN = 1024
 EPS = 1e-05
 THETA = 160000.0
+
+
+def attach_frame_by_axis(xs):
+    net_axis = "tensor"
+    ndev = lax.psum(1, axis_name=net_axis)
+    side_arr = list(map(lambda kk: (kk - 1, kk), range(1, ndev))) + [(ndev - 1, 0)]
+    w_next = xs
+    seen = [w_next]
+    for _ in range(ndev - 1):
+        w_next = lax.ppermute(w_next, axis_name=net_axis, perm=side_arr)
+        seen += [w_next]
+    return jnp.roll(
+        jnp.concatenate([*reversed(seen)], axis=0),
+        shift=(lax.axis_index(net_axis) + 1) * w_next.shape[0],
+        axis=0,
+    )
 
 
 def layer_norm(values, gain):
@@ -173,7 +189,7 @@
     gain_one = gain_first.astype(jnp.float32)
     gain_two = gain_second.astype(jnp.float32)
     grad_top = grad_output.astype(jnp.float32)
-    grad_all = lax.all_gather(grad_output, "tensor", axis=0, tiled=True)
+    grad_all = attach_frame_by_axis(grad_output)
     grad_down = jnp.einsum("tf,td->fd", hidden, grad_all, preferred_element_type=jnp.float32)
     grad_hidden = jnp.einsum("td,fd->tf", grad_all, down_w, preferred_element_type=jnp.float32)
     geglu_pull = jax.vjp(geglu, pair)[1]

time: 1330 us -> 1260 us (0.947)
  waiting for transfers between devices: 989 us -> 900 us
    ppermute x0 -> x3, waiting for transfers between devices: none -> 87.3 us  [attach_frame_by_axis(): w_next = lax.ppermute(w_next, axis_name=net_axis, perm=side_arr)]
    all_gather x1 -> x0, waiting for transfers between devices: 82.2 us -> none  [local(): grad_all = lax.all_gather(grad_output, 'tensor', axis=0, tiled=True)]
    all_gather x1, waiting for transfers between devices: 82.9 us -> 34.4 us  [local(): gathered_two = lax.all_gather(normed_two, 'tensor', axis=0, tiled=True)]
    all_gather x1, waiting for transfers between devices: 23.5 us -> 0.01 us  [local(): lax.all_gather(w_down, 'dp', axis=1, tiled=True)]
    all_gather x1, waiting for transfers between devices: 23.2 us -> 0.01 us  [local(): lax.all_gather(w_in, 'dp', axis=0, tiled=True)]
  transfers between devices with their start and end apart: 15 -> 17, of which waited for: 15 -> 15; matrix products, arithmetic and copies ran while one was open for 5% -> 7% of each run, Pallas kernels for 0% -> 0%
where the time goes in v1:
time: 1260 us; the launch traced here: 1250 us
  waiting for transfers between devices  900 us (71%)
  matrix products  152 us (12%)
  other arithmetic  65.7 us (5%)
  blocking collectives  56.8 us (5%)
  local copies, waits for them, and re-layouts  38.3 us (3%)
  between operations  15.5 us (1%)
  starting transfers between devices  14.1 us (1%)
    reduce_scatter x1, waiting for transfers between devices, local(): lax.psum_scatter(jnp.dot(attended_b, out_w, preferred_element_type=jnp.fl...  133 us
    reduce_scatter x1, waiting for transfers between devices, local(): lax.psum_scatter(jnp.einsum('tcf,dcf->td', grad_pair, in_w, preferred_ele...  123 us
    reduce_scatter x1, waiting for transfers between devices, local(): lax.psum_scatter(jnp.einsum('tcf,dcf->td', grad_proj, qkv_w, preferred_el...  109 us
    ppermute x3, waiting for transfers between devices, attach_frame_by_axis(): w_next = lax.ppermute(w_next, axis_name=net_axis, perm=side_arr)  87.3 us
    all_gather x1, waiting for transfers between devices, local(): gathered_one = lax.all_gather(normed_one, 'tensor', axis=0, tiled=True)  83.2 us
    all_gather x1, waiting for transfers between devices, local(): grad_res_all = lax.all_gather(grad_res_b, 'tensor', axis=0, tiled=True)  81.4 us
    reduce_scatter x1, waiting for transfers between devices, local(): lax.psum_scatter(jnp.dot(hidden, down_w, preferred_element_type=jnp.float...  77 us
    reduce_scatter x1, waiting for transfers between devices, local(): lax.psum_scatter(grad_in, 'dp', scatter_dimension=0, tiled=True)  61.5 us
  transfers between devices with their start and end apart: 17, of which 15 were waited for; matrix products, arithmetic and copies ran while one was open for 7% of the time, Pallas kernels for 0%

profile of v1, /device:TPU:0, one launch (start us, length us, event | category | flops | bytes accessed | tf_op | source)
XLA Modules:
  0.0 1245.3 jit_solution(6675823136121205539)
XLA Ops:
  9.0 10.3 all-gather
  25.3 11.9 all_gather.36
  39.9 83.2 %all-gather.9.cloned.1.call-done = bf16[2048,1024]{1,0:T(8,128)(2,1)} async-done(((bf16[512,1024]{1,0:T(8,128)(2,1)}), bf16[2048,1024]{1,0:T(8,128)(2,1)}) %all-gather.9.cloned.1.call-update) | async-done | bytes 4194320 | tf_op jit(solution)/shard_map/all_gather | solution.py:151
  130.3 29.7 %while.33 = (s32[]{:T(128)}, bf16[4,512,4,64]{1,3,2,0:T(8,128)(2,1)}, f32[4,4,512]{2,1,0:T(4,128)S(1)}, s32[4]{0:T(128)S(1)}, bf16[2048,4,64]{0,2,1:T(8,128)(2,1...) while((s32[]{:T(128)}, ...), condition=%wide.region_5.6_spmd, body=%wide.region_2.5_spmd.sunk | while | flops 553646080 | bytes 35455444 | solution.py:79
  179.7 133.2 %reduce-scatter.9.cloned.1.call-done = f32[512,1024]{1,0:T(8,128)} async-done(((f32[2048,1024]{1,0:T(8,128)}), f32[512,1024]{1,0:T(8,128)}) %reduce-scatter.9.cloned.1.call-update) | async-done | bytes 2097168 | tf_op jit(solution)/shard_map/reduce_scatter | solution.py:162
  318.0 25.6 %collective-permute-done = bf16[512,1024]{1,0:T(8,128)(2,1)S(1)} collective-permute-done((bf16[512,1024]{1,0:T(8,128)(2,1)}, bf16[512,1024]{1,0:T(8,128)(2,1)S(1)}, u32[]{:S(2)}, u32[]{:S(2)}) %collective-permute-start) | collective-permute-done | bytes 1048608 | tf_op jit(solution)/shard_map/ppermute | solution.py:19
  344.6 25.7 %collective-permute-done.1 = bf16[512,1024]{1,0:T(8,128)(2,1)} collective-permute-done((bf16[512,1024]{1,0:T(8,128)(2,1)S(1)}, bf16[512,1024]{1,0:T(8,128)(2,1)}, u32[]{:S(2)}, u32[]{:S(2)}) %collective-permute-start.1) | collective-permute-done | bytes 1048608 | tf_op jit(solution)/shard_map/ppermute | solution.py:19
  370.6 36.0 %collective-permute-done.2 = bf16[512,1024]{1,0:T(8,128)(2,1)} collective-permute-done((bf16[512,1024]{1,0:T(8,128)(2,1)}, bf16[512,1024]{1,0:T(8,128)(2,1)}, u32[]{:S(2)}, u32[]{:S(2)}) %collective-permute-start.2) | collective-permute-done | bytes 1048608 | tf_op jit(solution)/shard_map/ppermute | solution.py:19
  429.3 34.4 %all-gather.13.cloned.1.call-done = bf16[2048,1024]{1,0:T(8,128)(2,1)} async-done(((bf16[512,1024]{1,0:T(8,128)(2,1)}), bf16[2048,1024]{1,0:T(8,128)(2,1)}) %all-gather.13.cloned.1.call-update) | async-done | bytes 4194320 | tf_op jit(solution)/shard_map/all_gather | solution.py:170
  472.3 12.5 %multiply_bitcast_fusion = (f32[2048,1,656]{0,2,1:T(8,128)}, f32[2048,656]{0,1:T(8,128)S(1)}) fusion(f32[2048,656]{0,1:T(8,128)S(1)} %copy-done.6, f32[2048,2,656]{0,2,1:T(8,128)S(1)} %fusion.66), kind=kLoop, calls=%fused_computation.65 | loop fusion | flops 87326720 | bytes 21495808 | tf_op jit(solution)/shard_map/transpose(jvp())/broadcast_in_dim | solution.py:50
  490.1 13.6 %convolution_bitcast_fusion.1 = f32[2048,1024]{1,0:T(8,128)} fusion(bf16[1024,2,656]{0,2,1:T(8,128)(2,1)} %all-gather.15.cloned.1.call-done, f32[2048,1,656]{0,2,1:T(8,128)} %get-tuple-element.379, f32[2048,1,656]{0,2,1:T(8,128)} %get-tuple-element.371), kind=kOutput, calls=%fused_computation.82 | convolution fusion | flops 5508300800 | bytes 21823488 | tf_op jit(solution)/shard_map/tcf,dcf->td/dot_general | solution.py:199
  503.6 11.9 reduce-scatter.11.cloned.1.call-start
  523.2 123.2 %reduce-scatter.13.cloned.1.call-done = f32[512,1024]{1,0:T(8,128)} async-done(((f32[2048,1024]{1,0:T(8,128)}), f32[512,1024]{1,0:T(8,128)}) %reduce-scatter.13.cloned.1.call-update) | async-done | bytes 2097168 | tf_op jit(solution)/shard_map/reduce_scatter | solution.py:198
  649.3 77.0 %reduce-scatter.11.cloned.1.call-done = bf16[512,1024]{1,0:T(8,128)(2,1)} async-done(((bf16[2048,1024]{1,0:T(8,128)(2,1)}), bf16[512,1024]{1,0:T(8,128)(2,1)}) %reduce-scatter.11.cloned.1.call-update) | async-done | bytes 1048592 | tf_op jit(solution)/shard_map/reduce_scatter | solution.py:173
  732.6 81.4 %all-gather.19.cloned.1.call-done = bf16[2048,1024]{1,0:T(8,128)(2,1)} async-done(((bf16[512,1024]{1,0:T(8,128)(2,1)}), bf16[2048,1024]{1,0:T(8,128)(2,1)}) %all-gather.19.cloned.1.call-update) | async-done | bytes 4194320 | tf_op jit(solution)/shard_map/all_gather | solution.py:208
  822.0 53.8 %while.34 = (s32[]{:T(128)}, f32[2048,4,64]{0,2,1:T(8,128)}, f32[2048,4,64]{0,2,1:T(8,128)S(1)}, f32[2048,4,64]{0,2,1:T(8,128)}, bf16[2048,4,64]{0,2,1:T(8,128)(...) while((s32[]{:T(128)}, f32[2048,4,64]{0,2,1:T(8,128)}, ...), condition=%wide.region_15.16_spmd, body=%wide.region_13.15_spmd.sunk | while | flops 1368258560 | bytes 95478312 | solution.py:134
  901.2 11.3 fusion.64
  927.3 109.3 %reduce-scatter.15.cloned.1.call-done = f32[512,1024]{1,0:T(8,128)} async-done(((f32[2048,1024]{1,0:T(8,128)}), f32[512,1024]{1,0:T(8,128)}) %reduce-scatter.15.cloned.1.call-update) | async-done | bytes 2097168 | tf_op jit(solution)/shard_map/reduce_scatter | solution.py:226
  1041.2 13.7 %all-reduce.8 = (f32[1024]{0:T(1024)S(1)}, f32[1024]{0:T(1024)S(1)}) all-reduce(f32[1024]{0:T(1024)S(1)} %get-tuple-element.329, f32[1024]{0:T(1024)S(1)} %copy-done.34), channel_id=10, replica_groups=mesh['dp'=8,'tensor'=4] {'dp'}, use_global_device_ids=true, to_apply=%region_24.25.clone | all-reduce | flops 2048 | bytes 16384
  1055.1 12.1 all-reduce.9
  1070.4 15.9 %reduce-scatter.23.cloned.1.call-done = f32[656,128]{1,0:T(8,128)} async-done(((f32[656,1024]{1,0:T(8,128)}), f32[656,128]{1,0:T(8,128)}) %reduce-scatter.23.cloned.1.call-update) | async-done | bytes 335888 | tf_op jit(solution)/shard_map/reduce_scatter | solution.py:239
  1086.4 61.5 %reduce-scatter.21.cloned.1.call-done = f32[128,2,656]{0,2,1:T(8,128)} async-done(((f32[1024,2,656]{0,2,1:T(8,128)}), f32[128,2,656]{0,2,1:T(8,128)}) %reduce-scatter.21.cloned.1.call-update) | async-done | bytes 671760 | tf_op jit(solution)/shard_map/reduce_scatter | solution.py:238
  1147.9 40.1 %reduce-scatter.19.cloned.1.call-done = f32[256,128]{1,0:T(8,128)} async-done(((f32[256,1024]{1,0:T(8,128)}), f32[256,128]{1,0:T(8,128)}) %reduce-scatter.19.cloned.1.call-update) | async-done | bytes 131088 | tf_op jit(solution)/shard_map/reduce_scatter | solution.py:237
  1188.0 50.5 %reduce-scatter.17.cloned.1.call-done = f32[128,3,256]{2,0,1:T(8,128)} async-done(((f32[1024,3,256]{2,0,1:T(8,128)}), f32[128,3,256]{2,0,1:T(8,128)}) %reduce-scatter.17.cloned.1.call-update) | async-done | bytes 393232 | tf_op jit(solution)/shard_map/reduce_scatter | solution.py:236
  (259 shorter events, 232.5 us)
Async XLA Ops:
  7.2 32.8 %all-gather.11.cloned.1.call-start = ((), (), s32[]{:S(2)}) async-start(), calls=%async_computation.9 | async-start | bytes 1769472 | tf_op jit(solution)/shard_map/all_gather | solution.py:139
  9.0 114.1 %all-gather.9.cloned.1.call-start = ((), (), s32[]{:S(2)}) async-start(), calls=%async_computation.8 | async-start | bytes 5242880 | tf_op jit(solution)/shard_map/all_gather | solution.py:151
  25.1 287.8 %reduce-scatter.9.cloned.1.call-start = ((), (), s32[]{:S(2)}) async-start(), calls=%async_computation.10 | async-start | bytes 10485760 | tf_op jit(solution)/shard_map/reduce_scatter | solution.py:162
  169.8 251.5 %all-gather.17.cloned.1.call-start = ((), (), s32[]{:S(2)}) async-start(), calls=%async_computation.13 | async-start | bytes 1511424 | tf_op jit(solution)/shard_map/all_gather | solution.py:142
  170.3 258.9 %all-gather.15.cloned.1.call-start = ((), (), s32[]{:S(2)}) async-start(), calls=%async_computation.12 | async-start | bytes 3022848 | tf_op jit(solution)/shard_map/all_gather | solution.py:141
  170.9 292.8 %all-gather.13.cloned.1.call-start = ((), (), s32[]{:S(2)}) async-start(), calls=%async_computation.11 | async-start | bytes 5242880 | tf_op jit(solution)/shard_map/all_gather | solution.py:170
  316.7 329.7 %reduce-scatter.13.cloned.1.call-start = ((), (), s32[]{:S(2)}) async-start(), calls=%async_computation.15 | async-start | bytes 10485760 | tf_op jit(solution)/shard_map/reduce_scatter | solution.py:198
  316.8 26.8 %collective-permute-start = (bf16[512,1024]{1,0:T(8,128)(2,1)}, bf16[512,1024]{1,0:T(8,128)(2,1)S(1)}, u32[]{:S(2)}, u32[]{:S(2)}) collective-permute-start(bf16[512,1024]{1,0:T(8,128)(2,1)} %param.19), channel_id=1, source_target_pairs={{0,1},{1,2},{2,3},{3,0},{4,5},{5,6},{6,7},{7,4},{8,9},{9,10},{10,1... | collective-permute-start | bytes 3145736 | tf_op jit(solution)/shard_map/ppermute | solution.py:19
  344.6 25.7 %collective-permute-start.1 = (bf16[512,1024]{1,0:T(8,128)(2,1)S(1)}, bf16[512,1024]{1,0:T(8,128)(2,1)}, u32[]{:S(2)}, u32[]{:S(2)}) collective-permute-start(bf16[512,1024]{1,0:T(8,128)(2,1)S(1)} %collective-permute-done), channel_id=1, source_target_pairs={{0,1},{1,2},{2,3},{3,0},{4,5},{5,6},{6,7},{7,4},{8,9},{9,10},{10,1... | collective-permute-start | bytes 3145736 | tf_op jit(solution)/shard_map/ppermute | solution.py:19
  370.3 36.2 %collective-permute-start.2 = (bf16[512,1024]{1,0:T(8,128)(2,1)}, bf16[512,1024]{1,0:T(8,128)(2,1)}, u32[]{:S(2)}, u32[]{:S(2)}) collective-permute-start(bf16[512,1024]{1,0:T(8,128)(2,1)} %collective-permute-done.1), channel_id=1, source_target_pairs={{0,1},{1,2},{2,3},{3,0},{4,5},{5,6},{6,7},{7,4},{8,9},{9,10},{10,1... | collective-permute-start | bytes 3145736 | tf_op jit(solution)/shard_map/ppermute | solution.py:19
  503.6 222.6 %reduce-scatter.11.cloned.1.call-start = ((), (), s32[]{:S(2)}) async-start(), calls=%async_computation.14 | async-start | bytes 5242880 | tf_op jit(solution)/shard_map/reduce_scatter | solution.py:173
  523.2 290.9 %all-gather.19.cloned.1.call-start = ((), (), s32[]{:S(2)}) async-start(), calls=%async_computation.16 | async-start | bytes 5242880 | tf_op jit(solution)/shard_map/all_gather | solution.py:208
  732.6 304.0 %reduce-scatter.15.cloned.1.call-start = ((), (), s32[]{:S(2)}) async-start(), calls=%async_computation.17 | async-start | bytes 10485760 | tf_op jit(solution)/shard_map/reduce_scatter | solution.py:226
  893.4 193.0 %reduce-scatter.23.cloned.1.call-start = ((), (), s32[]{:S(2)}) async-start(), calls=%async_computation.21 | async-start | bytes 3022848 | tf_op jit(solution)/shard_map/reduce_scatter | solution.py:239
  901.1 246.7 %reduce-scatter.21.cloned.1.call-start = ((), (), s32[]{:S(2)}) async-start(), calls=%async_computation.20 | async-start | bytes 6045696 | tf_op jit(solution)/shard_map/reduce_scatter | solution.py:238
  912.5 275.5 %reduce-scatter.19.cloned.1.call-start = ((), (), s32[]{:S(2)}) async-start(), calls=%async_computation.19 | async-start | bytes 1179648 | tf_op jit(solution)/shard_map/reduce_scatter | solution.py:237
  918.2 118.4 %copy-start = (bf16[512,1024]{1,0:T(8,128)(2,1)S(1)}, bf16[512,1024]{1,0:T(8,128)(2,1)}, u32[]{:S(2)}) copy-start(bf16[512,1024]{1,0:T(8,128)(2,1)} %param.12) | copy-start | bytes 3145732
  918.2 118.4 %copy-start.26 = (f32[8,1,128]{2,1,0:T(1,128)S(1)}, f32[8,1,128]{2,1,0:T(1,128)}, u32[]{:S(2)}) copy-start(f32[8,1,128]{2,1,0:T(1,128)} %copy-done.25) | copy-start | bytes 12292
  918.2 118.4 %copy-start.28 = (f32[512]{0:T(512)S(1)}, f32[512]{0:T(512)}, u32[]{:S(2)}) copy-start(f32[512]{0:T(512)} %copy-done.27) | copy-start | bytes 6148
  918.2 320.2 %reduce-scatter.17.cloned.1.call-start = ((), (), s32[]{:S(2)}) async-start(), calls=%async_computation.18 | async-start | bytes 3538944 | tf_op jit(solution)/shard_map/reduce_scatter | solution.py:236
  926.0 112.7 %copy-start.33 = (f32[512]{0:T(512)S(1)}, f32[512]{0:T(512)}, u32[]{:S(2)}) copy-start(f32[512]{0:T(512)} %copy-done.32) | copy-start | bytes 6148
  926.0 112.7 %copy-start.31 = (f32[512]{0:T(512)S(1)}, f32[512]{0:T(512)}, u32[]{:S(2)}) copy-start(f32[512]{0:T(512)} %copy-done.30) | copy-start | bytes 6148
  926.0 115.3 %copy-start.34 = (f32[1024]{0:T(1024)S(1)}, f32[1024]{0:T(1024)}, u32[]{:S(2)}) copy-start(f32[1024]{0:T(1024)} %get-tuple-element.327) | copy-start | bytes 12292
  926.0 141.2 %copy-start.8 = (f32[512,1024]{1,0:T(8,128)S(1)}, f32[512,1024]{1,0:T(8,128)}, u32[]{:S(2)}) copy-start(f32[512,1024]{1,0:T(8,128)} %copy-done.7) | copy-start | bytes 6291460
  (48 other events, 391.2 us)
Sparse Core Ops, SparseCore 0:
  10.5 29.4 all-gather.10
  42.1 80.9 all-gather.8
  169.9 142.9 reduce-scatter.8
  314.6 25.5 all-gather.16
  342.0 30.7 all-gather.14
  374.8 88.8 all-gather.12
  503.8 142.6 reduce-scatter.12
  648.7 77.4 reduce-scatter.10
  732.7 81.2 all-gather.18
  893.5 142.9 reduce-scatter.14
  1041.0 45.3 reduce-scatter.22
  1090.6 57.2 reduce-scatter.20
  1151.9 35.9 reduce-scatter.18
  1192.2 46.2 reduce-scatter.16
